TPU v7x, 128 devices: a whole 4x4x4 slice. The times are simulated.
128 devices in a mesh: row: 8 (over x, core), col: 16 (over z, y).
Axes of the slice: x: 4, y: 4, z: 4, core: 2. Of those that a mesh axis runs over, the one named last changes fastest.
Arguments:
- child_update: bfloat16 [16, 8, 128, 8, 16, 128], P(None, 'row', None, None, 'col'), may hold values from -6 to 6
- child_panel: bfloat16 [16, 8, 128, 512], P(None, 'row', None, 'col'), may hold values from -1.1953125 to 1.1953125
- front: bfloat16 [24, 8, 128, 12, 16, 128], P(None, 'row', None, None, 'col'), may hold values from -6 to 6
- diag_inverse: bfloat16 [512, 512], replicated, may hold values from -0.0625 to 0.0625
- parent_tile: int32 [128], replicated, may hold values from 0 to 191, as said below
Outputs:
- panel: bfloat16 [24, 8, 128, 16, 32], P(None, 'row', None, 'col')
- updated_front: bfloat16 [24, 8, 128, 12, 16, 128], P(None, 'row', None, None, 'col')
Inputs may be any that keep to these rules, and one draw needn't show every extreme that they name: `parent_tile`: all values are distinct. Tile t lives on process row t mod 8 and process column t mod 16. The child tiles of one process row (equal a mod 8) send exactly 2 to each process row; the child tiles of one process column (equal a mod 16) send at most 1 to any process column, and exactly 1 to some.
All inputs are finite; a program needn't handle non-finite values.
Results may differ from a plain program's by a relative error of at most 0.0068.
Values may be sent and summed in bfloat16 or wider, within the bound.
A program may use at most 256 MiB of HBM per device.

v0:
```python
import jax
import jax.numpy as jnp
from jax import lax
from jax.sharding import PartitionSpec as P


def spread(value, axis, source):
    kept = jnp.where(lax.axis_index(axis) == source, value, 0).astype(value.dtype)
    return lax.psum(kept, axis)


def tile_ranks(group, target, order):
    same = (
        (group[:, None] == group[None, :])
        & (target[:, None] == target[None, :])
        & (order[None, :] < order[:, None])
    )
    return jnp.sum(same.astype(jnp.int32), axis=1)


def pick_index(matches, values):
    return jnp.sum(jnp.where(matches, values[None, :], 0), axis=1)


def column_owned(rows, tile_size, fold_ratio, parity):
    grouped = rows.reshape(
        rows.shape[0] // (tile_size * fold_ratio), fold_ratio, tile_size, rows.shape[1]
    )
    chosen = lax.dynamic_index_in_dim(grouped, parity, axis=1, keepdims=False)
    return chosen.reshape(-1, rows.shape[1])


def body(child_update, child_panel, front, diag_inverse, parent_tile):
    row_count = lax.axis_size("row")
    col_count = lax.axis_size("col")
    row_index = lax.axis_index("row")
    col_index = lax.axis_index("col")
    tile_size = front.shape[2]
    child_rows = child_update.shape[0]
    child_cols = child_update.shape[3]
    parent_rows = front.shape[0]
    parent_cols = front.shape[3]
    panel_width = diag_inverse.shape[0]
    panel_tiles = panel_width // tile_size
    fold_ratio = col_count // row_count
    parity = col_index // row_count % fold_ratio
    root_row = col_index % row_count
    tile_count = parent_tile.shape[0]
    row_slots = child_rows // row_count
    col_slots = max(1, tile_count // (col_count * col_count))
    own_panel = child_panel.reshape(child_rows * tile_size, child_panel.shape[3])
    full_rows = lax.all_gather(own_panel, "col", axis=1, tiled=True)
    across = spread(column_owned(full_rows, tile_size, fold_ratio, parity), "row", root_row)
    initial = child_update.reshape(child_rows * tile_size, child_cols * tile_size).astype(
        jnp.float32
    )
    product_child = lax.dot_general(
        full_rows, across, (((1,), (1,)), ((), ())), preferred_element_type=jnp.float32
    )
    schur = (initial - product_child).astype(jnp.bfloat16)
    child_ids = jnp.arange(tile_count, dtype=jnp.int32)
    owner_col = parent_tile % col_count
    owner_row = owner_col % row_count
    row_rank = tile_ranks(child_ids % row_count, owner_row, child_ids // row_count)
    col_rank = tile_ranks(child_ids % col_count, owner_col, child_ids // col_count)
    row_slot = owner_row * row_slots + row_rank
    col_slot = owner_col * col_slots + col_rank
    row_positions = jnp.arange(child_rows, dtype=jnp.int32)
    col_positions = jnp.arange(col_count * col_slots, dtype=jnp.int32)
    matches = ((child_ids % row_count)[None, :] == row_index) & (
        row_slot[None, :] == row_positions[:, None]
    )
    row_order = pick_index(matches, child_ids // row_count)
    matches = ((child_ids % col_count)[None, :] == col_index) & (
        col_slot[None, :] == col_positions[:, None]
    )
    col_valid = jnp.any(matches, axis=1)
    col_order = pick_index(matches, child_ids // col_count)
    arrival_row = child_ids % row_count * row_slots + row_rank
    matches = (owner_row[None, :] == row_index) & (arrival_row[None, :] == row_positions[:, None])
    row_target = pick_index(matches, parent_tile // row_count)
    arrival_col = child_ids % col_count * col_slots + col_rank
    matches = (owner_col[None, :] == col_index) & (arrival_col[None, :] == col_positions[:, None])
    col_target = jnp.where(
        jnp.any(matches, axis=1), pick_index(matches, parent_tile // col_count), parent_cols
    )
    ordered = jnp.take(
        schur.reshape(child_rows, tile_size, child_cols * tile_size), row_order, axis=0
    )
    blocks = ordered.reshape(child_rows, tile_size, child_cols, tile_size)
    taken = jnp.take(blocks, col_order, axis=2)
    outgoing = jnp.where(
        col_valid[None, None, :, None], taken, jnp.zeros((), jnp.bfloat16)
    ).reshape(row_count, row_slots * tile_size, col_count * col_slots * tile_size)
    arrived = lax.all_to_all(
        lax.all_to_all(outgoing, "row", split_axis=0, concat_axis=0, tiled=True),
        "col",
        split_axis=2,
        concat_axis=2,
        tiled=True,
    )
    arrived = arrived.reshape(child_rows, tile_size, col_count * col_slots, tile_size)
    placed_rows = (
        jnp.zeros((parent_rows, tile_size, col_count * col_slots, tile_size), jnp.float32)
        .at[row_target]
        .set(arrived.astype(jnp.float32))
    )
    placed = (
        jnp.zeros((parent_rows, tile_size, parent_cols, tile_size), jnp.float32)
        .at[:, :, col_target]
        .add(placed_rows, mode="drop")
    )
    extended = (
        front.reshape(parent_rows, tile_size, parent_cols, tile_size).astype(jnp.float32) + placed
    ).astype(jnp.bfloat16)
    extended_flat = extended.reshape(parent_rows * tile_size, parent_cols * tile_size)
    first_tile = extended_flat[:, :tile_size]
    inverse_rows = lax.dynamic_slice_in_dim(
        diag_inverse, jnp.minimum(col_index, panel_tiles - 1) * tile_size, tile_size, 0
    )
    own_term = jnp.dot(first_tile, inverse_rows, preferred_element_type=jnp.float32)
    own_term = jnp.where(col_index < panel_tiles, own_term, jnp.zeros((), jnp.float32))
    panel = lax.psum(own_term, "col").astype(jnp.bfloat16)
    crossing = spread(column_owned(panel, tile_size, fold_ratio, parity), "row", root_row)
    product = lax.dot_general(
        panel, crossing, (((1,), (1,)), ((), ())), preferred_element_type=jnp.float32
    )
    renewed = (
        (extended_flat.astype(jnp.float32) - product)
        .astype(jnp.bfloat16)
        .reshape(parent_rows, tile_size, parent_cols, tile_size)
    )
    row_tiles = row_index + row_count * jnp.arange(parent_rows, dtype=jnp.int32)
    col_tiles = col_index + col_count * jnp.arange(parent_cols, dtype=jnp.int32)
    trailing = (row_tiles[:, None, None, None] >= panel_tiles) & (
        col_tiles[None, None, :, None] >= panel_tiles
    )
    updated = jnp.where(trailing, renewed, extended)
    slice_width = panel_width // col_count
    own_columns = lax.dynamic_slice_in_dim(panel, col_index * slice_width, slice_width, 1)
    return (
        own_columns.reshape(parent_rows, 1, tile_size, 1, slice_width),
        updated.reshape(parent_rows, 1, tile_size, parent_cols, 1, tile_size),
    )


def solution(mesh):
    return jax.shard_map(
        body,
        mesh=mesh,
        in_specs=(
            P(None, "row", None, None, "col", None),
            P(None, "row", None, "col"),
            P(None, "row", None, None, "col", None),
            P(),
            P(),
        ),
        out_specs=(P(None, "row", None, "col", None), P(None, "row", None, None, "col", None)),
        check_vma=False,
    )
```

profile of v0, /device:TPU:1, one launch (start us, length us, event | category | flops | bytes accessed | tf_op | source)
XLA Modules:
  0.0 881.7 jit_solution(10036989844571629160)
XLA Ops:
  16.1 9.2 %copy.87 = f32[2048,1024]{0,1:T(8,128)} copy(f32[2048,1024]{1,0:T(8,128)} %bitcast.81) | data formatting | bytes 16777216 | tf_op jit(solution)/shard_map/convert_element_type | solution.py:54
  26.2 32.0 %all-gather.2.cloned.1.call-done = bf16[2048,512]{0,1:T(8,128)(2,1)} async-done(((bf16[2048,32]{0,1:T(8,128)(2,1)}), bf16[2048,512]{0,1:T(8,128)(2,1)}) %all-gather.2.cloned.1.call-update) | async-done | bytes 2097168 | tf_op jit(solution)/shard_map/all_gather | solution.py:52
  71.8 61.2 %all-reduce.4.cloned.1.call-done = bf16[1024,512]{1,0:T(8,128)(2,1)} async-done(((bf16[1024,512]{1,0:T(8,128)(2,1)}), bf16[1024,512]{1,0:T(8,128)(2,1)}) %all-reduce.4.cloned.1.call-update) | async-done | bytes 1048592 | tf_op jit(solution)/shard_map/psum | solution.py:9
  165.7 13.7 %copy.76 = bf16[16,128,16,128]{3,2,1,0:T(8,128)(2,1)} copy(bf16[16,128,16,128]{3,1,0,2:T(8,128)(2,1)} %bitcast.80) | data formatting | bytes 16777216 | tf_op jit(solution)/shard_map/jit(_take)/gather | solution.py:91
  179.3 13.3 %gather.15 = bf16[8,256,2048]{2,1,0:T(8,128)(2,1)} reshape(bf16[16,128,16,128]{3,2,1,0:T(8,128)(2,1)} %copy.76) | data formatting | bytes 16777216 | tf_op jit(solution)/shard_map/jit(_take)/gather | solution.py:91
  200.3 103.3 %all_to_all.10 = bf16[8,256,2048]{2,1,0:T(8,128)(2,1)} all-to-all(bf16[8,256,2048]{2,1,0:T(8,128)(2,1)} %select_select_fusion), channel_id=1, replica_groups=mesh['row'=8,'col'=16] {'row'}, dimensions={0} | all-to-all | bytes 16777216 | tf_op jit(solution)/shard_map/all_to_all | solution.py:96
  303.6 12.8 %copy.77 = bf16[8,256,2048]{1,0,2:T(8,128)(2,1)} copy(bf16[8,256,2048]{2,1,0:T(8,128)(2,1)} %all_to_all.10) | data formatting | bytes 16777216 | tf_op jit(solution)/shard_map/all_to_all | solution.py:96
  323.6 12.5 %bitcast_convert_fusion = f32[24,128,12,128]{3,1,2,0:T(8,128)} fusion(bf16[24,1,128,12,1,128]{5,2,4,3,1,0:T(8,128)(2,1)} %param.7), kind=kLoop, calls=%fused_computation.6 | loop fusion | flops 4718592 | bytes 28311552 | tf_op jit(solution)/shard_map/convert_element_type | solution.py:114
  336.1 109.0 %all-to-all-done.1 = bf16[8,256,2048]{1,0,2:T(8,128)(2,1)} async-done(((bf16[8,256,2048]{1,0,2:T(8,128)(2,1)}), bf16[8,256,2048]{1,0,2:T(8,128)(2,1)}, u32[]{:S(2)}, u32[]{:S(2)}) %all-to-all-start.1) | async-done | bytes 8388640 | tf_op jit(solution)/shard_map/all_to_all | solution.py:95
  445.1 13.9 %reshape.331 = f32[16,128,16,128]{1,0,3,2:T(8,128)} reshape(bf16[8,256,2048]{1,0,2:T(8,128)(2,1)} %all-to-all-done.1) | data formatting | bytes 25165824 | tf_op jit(solution)/shard_map/convert_element_type | solution.py:106
  459.0 21.5 %copy.89 = f32[16,128,16,128]{3,2,1,0:T(8,128)} copy(f32[16,128,16,128]{1,0,3,2:T(8,128)} %reshape.331) | data formatting | bytes 33554432 | tf_op jit(solution)/shard_map/convert_element_type | solution.py:106
  480.5 11.1 %broadcast_in_dim.137 = f32[24,128,16,128]{3,2,1,0:T(8,128)} broadcast(f32[]{:T(128)} %constant.186.clone.1), dimensions={} | broadcast | bytes 25165828 | tf_op jit(solution)/shard_map/broadcast_in_dim | solution.py:104
  491.6 30.2 %scatter_fusion = f32[24,128,16,128]{3,2,1,0:T(8,128)} fusion(f32[24,128,16,128]{3,2,1,0:T(8,128)} %broadcast_in_dim.137, s32[16]{0:T(128)S(1)} %fusion.13, f32[16,128,16,128]{3,2,1,0:T(8,128)} %copy.89), kind=kCustom, calls=%fused_computation.2 | custom fusion | bytes 50331712 | tf_op jit(solution)/shard_map/scatter | solution.py:106
  521.8 20.9 %copy.79 = f32[16,24,128,128]{3,2,1,0:T(8,128)} copy(f32[16,24,128,128]{3,0,2,1:T(8,128)} %bitcast.76) | data formatting | bytes 50331648 | tf_op jit(solution)/shard_map/scatter | solution.py:106
  542.7 42.7 %scatter_fusion.1 = f32[24,128,12,128]{3,1,2,0:T(8,128)} fusion(f32[24,128,12,128]{3,1,2,0:T(8,128)} %bitcast_convert_fusion, s32[16]{0:T(128)S(1)} %fusion.12, f32[16,24,128,128]{3,2,1,0:T(8,128)} %copy.79), kind=kCustom, calls=%fused_computation.3 | custom fusion | flops 6291456 | bytes 75497536 | tf_op jit(solution)/shard_map/scatter-add | solution.py:111
  585.4 10.1 %convert_element_type.52 = bf16[24,128,12,128]{3,1,2,0:T(8,128)(2,1)} convert(f32[24,128,12,128]{3,1,2,0:T(8,128)} %scatter_fusion.1) | non-fusion elementwise | flops 4718592 | bytes 28311552 | tf_op jit(solution)/shard_map/convert_element_type | solution.py:115
  595.5 13.2 %copy.80 = bf16[24,128,12,128]{1,0,3,2:T(8,128)(2,1)} copy(bf16[24,128,12,128]{3,1,2,0:T(8,128)(2,1)} %convert_element_type.52) | data formatting | bytes 18874368 | tf_op jit(solution)/shard_map/convert_element_type | solution.py:115
  608.7 9.9 %copy.106 = bf16[192,8,24,128]{3,1,2,0:T(8,128)(2,1)} copy(bf16[192,8,24,128]{3,2,1,0:T(8,128)(2,1)} %bitcast.79) | data formatting | bytes 18874368
  623.4 137.7 %all-reduce.7 = bf16[3072,512]{1,0:T(8,128)(2,1)} all-reduce(f32[3072,512]{1,0:T(8,128)} %convolution_select_fusion), channel_id=1, replica_groups=mesh['row'=8,'col'=16] {'col'}, use_global_device_ids=true, to_apply=%region_11.12 | all-reduce | flops 1572864 | bytes 9437184 | tf_op jit(solution)/shard_map/psum | solution.py:123
  763.9 12.7 %copy.82 = bf16[3072,1536]{1,0:T(8,128)(2,1)} copy(bf16[3072,1536]{0,1:T(8,128)(2,1)} %bitcast.78) | data formatting | bytes 18874368 | tf_op jit(solution)/shard_map/reshape | solution.py:116
  778.9 52.5 %all-reduce.6.cloned.1.call-done = bf16[1536,512]{1,0:T(8,128)(2,1)} async-done(((bf16[1536,512]{1,0:T(8,128)(2,1)}), bf16[1536,512]{1,0:T(8,128)(2,1)}) %all-reduce.6.cloned.1.call-update) | async-done | bytes 1572880 | tf_op jit(solution)/shard_map/psum | solution.py:9
  831.4 10.8 %subtract_convert_fusion = bf16[3072,1536]{1,0:T(8,128)(2,1)} fusion(bf16[3072,1536]{1,0:T(8,128)(2,1)} %copy.82, bf16[3072,512]{1,0:T(8,128)(2,1)} %all-reduce.7, bf16[1536,512]{1,0:T(8,128)(2,1)} %all-reduce.6.cloned.1.call-done), kind=kOutput, calls=%fused_computation.4 | convolution fusion | flops 4845993984 | bytes 23592960 | tf_op jit(solution)/shard_map/dot_general | solution.py:125
  842.2 17.8 %reshape.332 = bf16[24,128,12,128]{3,2,1,0:T(8,128)(2,1)} reshape(bf16[3072,1536]{1,0:T(8,128)(2,1)} %subtract_convert_fusion) | data formatting | bytes 18874368 | tf_op jit(solution)/shard_map/reshape | solution.py:131
  860.0 15.2 %fusion = bf16[24,1,128,12,1,128]{5,2,4,3,1,0:T(8,128)(2,1)} fusion(bf16[24,128,12,128]{3,2,1,0:T(8,128)(2,1)} %reshape.332, pred[24,12]{1,0:T(8,128)(4,1)S(1)} %broadcast_and_fusion, f32[24,128,12,128]{3,1,2,0:T(8,128)} %scatter_fusion.1), kind=kLoop, calls=%fused_computation.8 | loop fusion | flops 9437184 | bytes 37749024
  (57 shorter events, 80.7 us)
Async XLA Ops:
  7.2 611.4 %copy-start = (bf16[512,512]{1,0:T(8,128)(2,1)S(1)}, bf16[512,512]{1,0:T(8,128)(2,1)}, u32[]{:S(2)}) copy-start(bf16[512,512]{1,0:T(8,128)(2,1)} %param.8) | copy-start | bytes 1572868
  7.2 51.0 %all-gather.2.cloned.1.call-start = ((), (), s32[]{:S(2)}) async-start(), calls=%async_computation.2 | async-start | bytes 2228224 | tf_op jit(solution)/shard_map/all_gather | solution.py:52
  8.9 124.1 %all-reduce.4.cloned.1.call-start = ((), (), s32[]{:S(2)}) async-start(), calls=%async_computation.3 | async-start | bytes 2097152 | tf_op jit(solution)/shard_map/psum | solution.py:9
  16.1 9.2 %copy-start.1 = (s32[128]{0:T(128)S(1)}, s32[128]{0:T(128)}, u32[]{:S(2)}) copy-start(s32[128]{0:T(128)} %param.9) | copy-start | bytes 1540
  316.4 128.7 %all-to-all-start.1 = ((bf16[8,256,2048]{1,0,2:T(8,128)(2,1)}), bf16[8,256,2048]{1,0,2:T(8,128)(2,1)}, u32[]{:S(2)}, u32[]{:S(2)}) async-start(bf16[8,256,2048]{1,0,2:T(8,128)(2,1)} %copy.77), calls=%async_computation.1 | async-start | bytes 16777216 | tf_op jit(solution)/shard_map/all_to_all | solution.py:95
  323.2 508.2 %all-reduce.6.cloned.1.call-start = ((), (), s32[]{:S(2)}) async-start(), calls=%async_computation.4 | async-start | bytes 3145728 | tf_op jit(solution)/shard_map/psum | solution.py:9
Sparse Core Ops, SparseCore 0:
  10.7 47.4 all-gather.1
  71.8 61.1 all-reduce.3
  763.9 67.4 all-reduce.5
where the time goes:
time: 886 us; the launch traced here: 882 us
  waiting for transfers between devices  255 us (29%)
  local copies, waits for them, and re-layouts  242 us (27%)
  blocking collectives  241 us (27%)
  other arithmetic  98.5 us (11%)
  matrix products  24.2 us (3%)
  between operations  13.9 us (2%)
    psum x1, blocking collectives, body(): panel = lax.psum(own_term, 'col').astype(jnp.bfloat16)  138 us
    psum x2, waiting for transfers between devices, spread(): return lax.psum(kept, axis)  114 us
    all_to_all x1, waiting for transfers between devices, body(): lax.all_to_all(lax.all_to_all(outgoing, 'row', split_axis=0, concat_axis=...  109 us
    all_to_all x1, blocking collectives, body(): lax.all_to_all(outgoing, 'row', split_axis=0, concat_axis=0, tiled=True)  103 us
    scatter x2, local copies, waits for them, and re-layouts, body(): placed_rows = jnp.zeros((parent_rows, tile_size, col_count * col_slots, t...  51.1 us
    scatter-add x1, other arithmetic, body(): placed = jnp.zeros((parent_rows, tile_size, parent_cols, tile_size), jnp....  42.7 us
    convert_element_type x2, local copies, waits for them, and re-layouts, body(): arrived.astype(jnp.float32)  35.4 us
    gather x3, local copies, waits for them, and re-layouts, body(): taken = jnp.take(blocks, col_order, axis=2)  34 us
  transfers between devices with their start and end apart: 4, of which 4 were waited for; matrix products, arithmetic and copies ran while one was open for 5% of the time, Pallas kernels for 0%

commit v1 on v0

v1 whole, which is shorter than its diff:
```python
import jax
import jax.numpy as jnp
from jax import lax
from jax.experimental import pallas as pl
from jax.experimental.pallas import tpu as pltpu
from jax.sharding import PartitionSpec as P

MESH = pl.DeviceIdType.MESH
BF = jnp.bfloat16
F32 = jnp.float32
ROWS = [(1, 0), (3, 0), (1, 1), (3, 1), (2, 0), (2, 1), (0, 1)]
RING = [1, 3, 2]
N_SEMS = 240


def tables(parent_tile, row, col):
    ids = jnp.arange(128, dtype=jnp.int32)
    mine_rows = lax.dynamic_index_in_dim(parent_tile.reshape(16, 8), row, 1, keepdims=False) % 8
    slots = jnp.arange(16, dtype=jnp.int32)
    to_row = mine_rows[None, :] == jnp.arange(8, dtype=jnp.int32)[:, None]
    first = jnp.min(jnp.where(to_row, slots[None, :], 15), axis=1)
    last = jnp.max(jnp.where(to_row, slots[None, :], 0), axis=1)
    row_order = jnp.stack([first, last], axis=1).reshape(16)
    mine_cols = lax.dynamic_index_in_dim(parent_tile.reshape(8, 16), col, 1, keepdims=False) % 16
    to_col = mine_cols[None, :] == slots[:, None]
    col_order = jnp.sum(jnp.where(to_col, jnp.arange(8, dtype=jnp.int32)[None, :], 0), axis=1)
    here = parent_tile % 8 == row
    lowest = jnp.min(jnp.where(here, ids, 999).reshape(16, 8), axis=0)
    rank = (ids.reshape(16, 8) != lowest[None, :]).reshape(128).astype(jnp.int32)
    row_match = parent_tile[None, :] == (row + 8 * jnp.arange(24, dtype=jnp.int32))[:, None]
    row_from = jnp.sum(jnp.where(row_match, (rank * 8 + ids % 8)[None, :], 0), axis=1)
    row_ok = jnp.any(row_match, axis=1).astype(jnp.int32)
    col_match = parent_tile[None, :] == (col + 16 * jnp.arange(12, dtype=jnp.int32))[:, None]
    col_from = jnp.sum(jnp.where(col_match, (ids % 16)[None, :], 0), axis=1)
    col_ok = jnp.any(col_match, axis=1).astype(jnp.int32)
    return jnp.concatenate([row_order, col_order, row_from, row_ok, col_from, col_ok]).astype(jnp.int32)


T_COL, T_RFROM, T_ROK, T_CFROM, T_COK = 16, 32, 56, 80, 92


def arrived_tile(tab, arr, i, j):
    source_row = tab[T_RFROM + i]
    rank, q = source_row // 8, source_row % 8
    half, place = q // 4, q % 4
    source = tab[T_CFROM + j]
    lo, hi = source // 4, source % 4
    major = jnp.where(half == 0, hi, lo)
    minor = jnp.where(half == 0, lo, hi)
    upper = arr[rank * 2, half, major, minor, place]
    lower = arr[rank * 2 + 1, half, major, minor, place]
    ok = (tab[T_ROK + i] * tab[T_COK + j]) == 1
    tile = jnp.concatenate([upper, lower], axis=0).astype(F32)
    return jnp.where(ok, tile, jnp.zeros_like(tile))


def exchange(
    tab, u, gt, front, dinv, arr_out, prow, pcol,
    us, ux, g1s, g1r, rowg, rowt, cmid, colt, colgr, colga, colgb, uf, sc, s1, mid, arr, fp, extc, eq, ep,
    lsem, ssem, rsem,
):
    r, c = lax.axis_index("row"), lax.axis_index("col")
    x, k, z, y = r // 2, r % 2, c // 4, c % 4
    counter = [0]
    pending = []

    def row_dev(dx, dk):
        return ((x + dx) % 4) * 2 + (k + dk) % 2

    def row_from(dx, dk):
        return ((x + 4 - dx) % 4) * 2 + (k + dk) % 2

    def sem():
        counter[0] += 1
        return counter[0] - 1

    def send(src, dst, dev, landing):
        n = sem()
        out = pltpu.make_async_remote_copy(src, dst, ssem.at[n], rsem.at[n], device_id=dev, device_id_type=MESH)
        out.start()
        pending.append(out)
        return pltpu.make_async_remote_copy(landing, landing, ssem.at[n], rsem.at[n], device_id=dev, device_id_type=MESH)

    def arrive(waits):
        for w in waits:
            w.wait_recv()

    def local(src, dst):
        n = sem()
        copy = pltpu.make_async_copy(src, dst, lsem.at[n])
        copy.start()
        return copy

    def to_z(d):
        return (r, ((z + d) % 4) * 4 + y)

    def to_y(d):
        return (r, z * 4 + (y + d) % 4)

    for rp in range(8):
        g1s[rp, 0] = gt[tab[2 * rp]]
        g1s[rp, 1] = gt[tab[2 * rp + 1]]
        g1s[rp, 2] = gt[2 * rp]
        g1s[rp, 3] = gt[2 * rp + 1]

    barrier = pltpu.get_barrier_semaphore()
    for dx, dk in ROWS:
        pl.semaphore_signal(barrier, inc=1, device_id=(row_dev(dx, dk), c), device_id_type=MESH)
    for d in RING:
        pl.semaphore_signal(barrier, inc=1, device_id=to_z(d), device_id_type=MESH)
        pl.semaphore_signal(barrier, inc=1, device_id=to_y(d), device_id_type=MESH)
    pl.semaphore_wait(barrier, 13)

    g1 = [
        send(g1s.at[row_dev(dx, dk)], g1r.at[r], (row_dev(dx, dk), c), g1r.at[row_from(dx, dk)])
        for dx, dk in ROWS
    ]
    g1r[r] = g1s[r]

    @pl.loop(0, 16)
    def _(n):
        us[n // 2, n % 2] = u[tab[n]]

    ux[r] = us[r]

    def send_child(part):
        rank, rows = part // 2, pl.ds((part % 2) * 512, 512)
        return [
            send(
                us.at[row_dev(dx, dk), rank, rows], ux.at[r, rank, rows], (row_dev(dx, dk), c),
                ux.at[row_from(dx, dk), rank, rows],
            )
            for dx, dk in ROWS
        ]

    child = {0: send_child(0)}
    copies = []

    arrive(g1)
    yz, zy = pl.ds((y * 4 + z) * 32, 32), pl.ds((z * 4 + y) * 32, 32)

    def col_piece(zp):
        return g1r.at[pl.ds(4 * (zp % 2), 4), 2 + zp // 2]

    c1 = [send(col_piece((z + d) % 4), cmid.at[z], to_z(d), cmid.at[(z + 4 - d) % 4]) for d in RING]
    own = [
        local(col_piece(z), cmid.at[z]),
        local(g1r.at[:, 0], rowg.at[0, :, yz]),
        local(g1r.at[:, 1], rowg.at[1, :, zy]),
    ]
    a1 = [
        send(g1r.at[:, 0], rowg.at[0, :, yz], to_z(d), rowg.at[0, :, pl.ds((y * 4 + (z + 4 - d) % 4) * 32, 32)])
        for d in RING
    ]
    b1 = [
        send(g1r.at[:, 1], rowg.at[1, :, zy], to_y(d), rowg.at[1, :, pl.ds((z * 4 + (y + 4 - d) % 4) * 32, 32)])
        for d in RING
    ]
    for copy in own:
        copy.wait()
    arrive(c1)
    c2 = [send(cmid.at[:, (y + d) % 4], colt.at[y], to_y(d), colt.at[(y + 4 - d) % 4]) for d in RING]
    mine = local(cmid.at[:, y], colt.at[y])
    arrive(a1)
    y128, z128 = pl.ds(y * 128, 128), pl.ds(z * 128, 128)
    a2 = [
        send(rowg.at[0, :, y128], rowg.at[0, :, y128], to_y(d), rowg.at[0, :, pl.ds((y + 4 - d) % 4 * 128, 128)])
        for d in RING
    ]
    arrive(b1)
    b2 = [
        send(rowg.at[1, :, z128], rowg.at[1, :, z128], to_z(d), rowg.at[1, :, pl.ds((z + 4 - d) % 4 * 128, 128)])
        for d in RING
    ]
    mine.wait()
    arrive(c2)
    d1 = [send(colt, colgr.at[r], (row_dev(d, 0), c), colgr.at[row_from(d, 0)]) for d in RING]
    local(colt, colgr.at[r]).wait()
    arrive(d1)
    sibling = (row_dev(0, 1), c)
    d2 = [send(colgr.at[2 * q + k], colgr.at[2 * q + k], sibling, colgr.at[2 * q + 1 - k]) for q in range(4)]
    child[1] = send_child(1)
    arrive(d2)
    for j in range(8):
        for a in range(4):
            for b in range(4):
                piece = colgr[j, a, b]
                colga[pl.ds((a * 4 + b) * 32, 32), pl.ds(j * 128, 128)] = piece
                colgb[pl.ds((b * 4 + a) * 32, 32), pl.ds(j * 128, 128)] = piece

    def turn(rank):
        @pl.loop(0, 8)
        def _(q):
            turned = rowg[rank, q].T
            rowt[2 * rank, q] = turned[0:64]
            rowt[2 * rank + 1, q] = turned[64:128]

    def schur(part, half):
        rank = part // 2
        colg = colga if rank == 0 else colgb

        @pl.loop(0, 4)
        def _(q):
            uf[pl.ds(q * 512, 512)] = ux[half * 4 + q, rank, pl.ds((part % 2) * 512, 512)].astype(F32)

        left = rowt.at[part, pl.ds(half * 4, 4)]

        for n in range(4):
            prod = jnp.dot(
                left[...].reshape(256, 512), colg[:, n * 256 : n * 256 + 256], preferred_element_type=F32
            )
            for e in range(2):
                j = 2 * n + e
                sc[j] = (uf[pl.ds(j, 256, stride=8), :] - prod[:, e * 128 : e * 128 + 128]).astype(BF)

        @pl.loop(0, 16)
        def _(t):
            lo, hi = t // 4, t % 4
            if half == 0:
                s1[part, half, lo, hi] = sc[tab[T_COL + t]].reshape(4, 64, 128)
            else:
                s1[part, half, hi, lo] = sc[tab[T_COL + t]].reshape(4, 64, 128)

    def step_one(part, half):
        me, to = (z, to_z) if half == 0 else (y, to_y)
        waits = [
            send(s1.at[part, half, (me + d) % 4], mid.at[part, half, me], to(d), mid.at[part, half, (me + 4 - d) % 4])
            for d in RING
        ]
        return waits, local(s1.at[part, half, me], mid.at[part, half, me])

    def step_two(part, half, first):
        arrive(first[0])
        first[1].wait()
        me, to = (y, to_y) if half == 0 else (z, to_z)
        waits = [
            send(
                mid.at[part, half, :, (me + d) % 4], arr.at[part, half, me], to(d), arr.at[part, half, (me + 4 - d) % 4]
            )
            for d in RING
        ]
        copies.append(local(mid.at[part, half, :, me], arr.at[part, half, me]))
        return waits

    one, two = {}, []
    for part in range(4):
        if part == 0:
            arrive(a2)
            turn(0)
        if part == 2:
            arrive(b2)
            turn(1)
        arrive(child[part])
        for half in range(2):
            schur(part, half)
            one[part, half] = step_one(part, half)
        if part + 2 < 4:
            child[part + 2] = send_child(part + 2)
        if part >= 1:
            for half in range(2):
                two += step_two(part - 1, half, one[part - 1, half])
    for half in range(2):
        two += step_two(3, half, one[3, half])

    @pl.when(z == 0)
    def _():
        copy = pltpu.make_async_copy(front.at[:, 0], fp, lsem.at[N_SEMS - 1])
        copy.start()
        copy.wait()

    arrive(two)
    for copy in copies:
        copy.wait()
    keep = local(arr, arr_out)

    lanes = pl.ds(pl.multiple_of(y * 128, 128), 128)
    spread_sems = [sem() for _ in range(4)]

    def spread(d):
        n = spread_sems[d]
        return pltpu.make_async_remote_copy(
            extc.at[d], eq, ssem.at[n], rsem.at[n], device_id=(r, 4 * d + y), device_id_type=MESH
        )

    @pl.when(z == 0)
    def _():
        @pl.loop(0, 24)
        def _(i):
            added = fp[i].astype(F32) + arrived_tile(tab, arr, i, 0)
            extc[i // 6, (i % 6) // 2, i % 2] = added.astype(BF)

        for d in (1, 2, 3):
            spread(d).start()
        eq[...] = extc[0]
        for d in (1, 2, 3):
            spread(d).wait_send()

    for d in (1, 2, 3):

        @pl.when(z == d)
        def _():
            spread(d).wait_recv()

    e1 = [
        send(
            eq.at[:, :, pl.ds((y + d) % 4 * 32, 32)], ep.at[:, :, :, lanes], to_y(d),
            ep.at[:, :, :, pl.ds(pl.multiple_of((y + 4 - d) % 4 * 128, 128), 128)],
        )
        for d in RING
    ]
    local(eq.at[:, :, pl.ds(y * 32, 32)], ep.at[:, :, :, lanes]).wait()
    arrive(e1)
    made = jnp.dot(ep[...].reshape(192, 512), dinv[...], preferred_element_type=F32).astype(BF)
    y32 = pl.ds(y * 32, 32)
    prow[z, :, :, y32] = made.reshape(3, 2, 32, 512)
    p1 = [
        send(prow.at[z, :, 0, y32], prow.at[z, :, 0, y32], to_z(d), prow.at[(z + 4 - d) % 4, :, 0, y32]) for d in RING
    ]
    p2 = [
        send(prow.at[z, :, 1, y32], prow.at[z, :, 1, y32], to_y(d), prow.at[z, :, 1, pl.ds((y + 4 - d) % 4 * 32, 32)])
        for d in RING
    ]
    arrive(p1)
    p3 = [
        send(prow.at[:, :, 0, y32], prow.at[:, :, 0, y32], to_y(d), prow.at[:, :, 0, pl.ds((y + 4 - d) % 4 * 32, 32)])
        for d in RING
    ]
    arrive(p2)
    p4 = [send(prow.at[z, :, 1], prow.at[z, :, 1], to_z(d), prow.at[(z + 4 - d) % 4, :, 1]) for d in RING]
    arrive(p3)
    arrive(p4)

    root = c % 8
    upper = c // 8
    n_in = sem()
    n_out = [sem() for _ in ROWS]

    def piece(q):
        return pl.ds(q * 16, 16)

    def deal(dx, dk, n):
        q = row_dev(dx, dk)
        return pltpu.make_async_remote_copy(
            prow.at[:, :, upper, piece(q)], pcol.at[:, :, piece(q)], ssem.at[n], rsem.at[n_in],
            device_id=(q, c), device_id_type=MESH,
        )

    @pl.when(r == root)
    def _():
        for (dx, dk), n in zip(ROWS, n_out):
            deal(dx, dk, n).start()
        copy = pltpu.make_async_copy(prow.at[:, :, upper, piece(r)], pcol.at[:, :, piece(r)], lsem.at[N_SEMS - 2])
        copy.start()
        copy.wait()
        for (dx, dk), n in zip(ROWS, n_out):
            deal(dx, dk, n).wait_send()

    @pl.when(r != root)
    def _():
        pltpu.make_async_remote_copy(
            pcol.at[:, :, piece(r)], pcol.at[:, :, piece(r)], ssem.at[n_in], rsem.at[n_in],
            device_id=(r, c), device_id_type=MESH,
        ).wait_recv()

    q1 = [
        send(
            pcol.at[:, :, piece(r)], pcol.at[:, :, piece(r)], (row_dev(d, 0), c), pcol.at[:, :, piece(row_from(d, 0))]
        )
        for d in RING
    ]
    arrive(q1)
    q2 = [
        send(
            pcol.at[:, :, piece(2 * q + k)], pcol.at[:, :, piece(2 * q + k)], sibling,
            pcol.at[:, :, piece(2 * q + 1 - k)],
        )
        for q in range(4)
    ]
    arrive(q2)
    keep.wait()
    for copy in pending:
        copy.wait_send()


def update(tab, front, arr, prow, pcol, out, panel):
    r, c = lax.axis_index("row"), lax.axis_index("col")
    step = pl.program_id(0)
    rows = prow[...].reshape(256, 512)
    pick = (lax.broadcasted_iota(jnp.int32, (32, 512), 1) - 32 * c) == lax.broadcasted_iota(jnp.int32, (32, 512), 0)
    chosen = lax.dot_general(
        jnp.where(pick, 1.0, 0.0).astype(BF), rows, (((1,), (1,)), ((), ())), preferred_element_type=F32
    ).astype(BF)
    panel[0] = chosen[:, 0:128]
    panel[1] = chosen[:, 128:256]
    for n in range(6):
        first, second = 2 * n, 2 * n + 1
        right = jnp.concatenate([pcol[first // 3, first % 3], pcol[second // 3, second % 3]], axis=0)
        prod = lax.dot_general(rows, right, (((1,), (1,)), ((), ())), preferred_element_type=F32)
        for e in range(2):
            j = 2 * n + e
            for b in range(2):
                i = 2 * step + b
                ext = (front[b, j].astype(F32) + arrived_tile(tab, arr, i, j)).astype(BF)
                new = (ext.astype(F32) - prod[b * 128 : b * 128 + 128, e * 128 : e * 128 + 128]).astype(BF)
                trailing = jnp.logical_and(r + 8 * i >= 4, c + 16 * j >= 4)
                out[b, j] = jnp.where(trailing, new, ext)


def body(child_update, child_panel, front, diag_inverse, parent_tile):
    row, col = lax.axis_index("row"), lax.axis_index("col")
    tab = tables(parent_tile, row, col)
    u = child_update.reshape(16, 1024, 128)
    gt = child_panel.reshape(16, 128, 32).transpose(0, 2, 1)
    tiles = front.reshape(24, 128, 12, 128).transpose(0, 2, 1, 3)
    vmem, anywhere = pl.BlockSpec(memory_space=pltpu.VMEM), pl.BlockSpec(memory_space=pl.ANY)
    smem = pl.BlockSpec(memory_space=pltpu.SMEM)
    arr, prow, pcol = pl.pallas_call(
        exchange,
        out_shape=(
            jax.ShapeDtypeStruct((4, 2, 4, 4, 4, 64, 128), BF),
            jax.ShapeDtypeStruct((4, 3, 2, 128, 512), BF),
            jax.ShapeDtypeStruct((4, 3, 128, 512), BF),
        ),
        in_specs=[smem, vmem, vmem, anywhere, vmem],
        out_specs=(anywhere, vmem, vmem),
        scratch_shapes=[
            pltpu.VMEM((8, 2, 1024, 128), BF),
            pltpu.VMEM((8, 2, 1024, 128), BF),
            pltpu.VMEM((8, 4, 32, 128), BF),
            pltpu.VMEM((8, 4, 32, 128), BF),
            pltpu.VMEM((2, 8, 512, 128), BF),
            pltpu.VMEM((4, 8, 64, 512), BF),
            pltpu.VMEM((4, 4, 32, 128), BF),
            pltpu.VMEM((4, 4, 32, 128), BF),
            pltpu.VMEM((8, 4, 4, 32, 128), BF),
            pltpu.VMEM((512, 1024), BF),
            pltpu.VMEM((512, 1024), BF),
            pltpu.VMEM((2048, 128), F32),
            pltpu.VMEM((8, 256, 128), BF),
            pltpu.VMEM((4, 2, 4, 4, 4, 64, 128), BF),
            pltpu.VMEM((4, 2, 4, 4, 4, 64, 128), BF),
            pltpu.VMEM((4, 2, 4, 4, 4, 64, 128), BF),
            pltpu.VMEM((24, 128, 128), BF),
            pltpu.VMEM((4, 3, 2, 128, 128), BF),
            pltpu.VMEM((3, 2, 128, 128), BF),
            pltpu.VMEM((3, 2, 32, 512), BF),
            pltpu.SemaphoreType.DMA((N_SEMS,)),
            pltpu.SemaphoreType.DMA((N_SEMS,)),
            pltpu.SemaphoreType.DMA((N_SEMS,)),
        ],
        compiler_params=pltpu.CompilerParams(collective_id=0, has_side_effects=True, vmem_limit_bytes=60 << 20),
        name="exchange",
    )(tab, u, gt, tiles, diag_inverse)
    updated, panel = pl.pallas_call(
        update,
        grid_spec=pltpu.PrefetchScalarGridSpec(
            num_scalar_prefetch=1,
            grid=(12,),
            in_specs=[
                pl.BlockSpec((2, 12, 128, 128), lambda s, t: (s, 0, 0, 0)),
                pl.BlockSpec((4, 2, 4, 4, 4, 64, 128), lambda s, t: (0, 0, 0, 0, 0, 0, 0)),
                pl.BlockSpec((1, 1, 2, 128, 512), lambda s, t: (s // 3, s % 3, 0, 0, 0)),
                pl.BlockSpec((4, 3, 128, 512), lambda s, t: (0, 0, 0, 0)),
            ],
            out_specs=[
                pl.BlockSpec((2, 12, 128, 128), lambda s, t: (s, 0, 0, 0)),
                pl.BlockSpec((2, 32, 128), lambda s, t: (s, 0, 0)),
            ],
        ),
        out_shape=(jax.ShapeDtypeStruct((24, 12, 128, 128), BF), jax.ShapeDtypeStruct((24, 32, 128), BF)),
        compiler_params=pltpu.CompilerParams(vmem_limit_bytes=60 << 20),
        name="update",
    )(tab, tiles, arr, prow, pcol)
    return (
        panel.transpose(0, 2, 1).reshape(24, 1, 128, 1, 32),
        updated.transpose(0, 2, 1, 3).reshape(24, 1, 128, 12, 1, 128),
    )


def solution(mesh):
    return jax.shard_map(
        body,
        mesh=mesh,
        in_specs=(
            P(None, "row", None, None, "col", None),
            P(None, "row", None, "col"),
            P(None, "row", None, None, "col", None),
            P(),
            P(),
        ),
        out_specs=(P(None, "row", None, "col", None), P(None, "row", None, None, "col", None)),
        check_vma=False,
    )
```

time: 886 us -> 234 us (0.26)
  waiting for transfers between devices: 255 us -> 0 us
  blocking collectives: 241 us -> 0 us
  local copies, waits for them, and re-layouts: 242 us -> 2.81 us
  Pallas kernels: 0 us -> 225 us
  other arithmetic: 98.5 us -> 4.39 us
  matrix products: 24.2 us -> 0 us
  between operations: 13.9 us -> 0.7 us
    pallas_call x0 -> x2, Pallas kernels: none -> 225 us  [the longest x1 205 us: body(): pl.pallas_call(exchange, out_shape=(jax.ShapeDtypeStruct((4, 2, 4, 4, 4,...]
    psum x1 -> x0, blocking collectives: 138 us -> none  [body(): panel = lax.psum(own_term, 'col').astype(jnp.bfloat16)]
    psum x2 -> x0, waiting for transfers between devices: 114 us -> none  [spread(): return lax.psum(kept, axis)]
    all_to_all x1 -> x0, waiting for transfers between devices: 109 us -> none  [body(): lax.all_to_all(lax.all_to_all(outgoing, 'row', split_axis=0, concat_axis=...]
    all_to_all x1 -> x0, blocking collectives: 103 us -> none  [body(): lax.all_to_all(outgoing, 'row', split_axis=0, concat_axis=0, tiled=True)]
    convert_element_type x4 -> x0, local copies, waits for them, and re-layouts: 57.8 us -> none  [the longest x2 35.4 us: body(): arrived.astype(jnp.float32)]
    scatter x2 -> x0, local copies, waits for them, and re-layouts: 51.1 us -> none  [body(): placed_rows = jnp.zeros((parent_rows, tile_size, col_count * col_slots, t...]
    scatter-add x1 -> x0, other arithmetic: 42.7 us -> none  [body(): placed = jnp.zeros((parent_rows, tile_size, parent_cols, tile_size), jnp....]
  transfers between devices with their start and end apart: 4 -> 0, of which waited for: 4 -> 0; matrix products, arithmetic and copies ran while one was open for 5% -> 0% of each run, Pallas kernels for 0% -> 0%
where the time goes in v1:
time: 234 us; the launch traced here: 233 us
  Pallas kernels  225 us (96%)
  other arithmetic  4.39 us (2%)
  local copies, waits for them, and re-layouts  2.81 us (1%)
    pallas_call x1, Pallas kernels, body(): pl.pallas_call(exchange, out_shape=(jax.ShapeDtypeStruct((4, 2, 4, 4, 4,...  205 us
    pallas_call x1, Pallas kernels, body(): pl.pallas_call(update, grid_spec=pltpu.PrefetchScalarGridSpec(num_scalar_...  19.8 us

profile of v1, /device:TPU:1, one launch (start us, length us, event | category | flops | bytes accessed | tf_op | source)
XLA Modules:
  0.0 233.0 jit_solution(14353214485002442636)
XLA Ops:
  0.7 0.8 compare_reduce_fusion
  1.5 0.8 compare_reduce_fusion.1
  2.4 0.7 and_select_fusion
  3.0 0.8 fusion.1
  3.9 0.7 reshape.142
  4.6 0.2 dynamic-slice_reduce_fusion.1
  4.8 0.1 select_reduce_fusion
  4.9 0.1 reshape.147
  5.0 0.1 mul.22
  5.1 0.8 fusion
  6.0 0.7 reshape.140
  6.7 0.2 dynamic-slice_reduce_fusion
  6.9 0.2 select_reduce_fusion.2
  7.1 0.1 copy.13
  7.2 0.1 reshape.141
  7.3 0.6 concatenate.3.tab
  7.9 205.3 %exchange.1 = (bf16[4,2,4,4,4,64,128]{6,5,4,3,2,1,0:T(8,128)(2,1)}, bf16[4,3,2,128,512]{4,3,2,1,0:T(8,128)(2,1)}, bf16[4,3,128,512]{3,2,1,0:T(8,128)(2,1)}) custom-call(s32[104]{0:T(128)} %concatenate.3.tab, bf16[16,1024,128]{2,1,0:T(8,128)(2,1)} %bitcast.21, bf16[16,32,128]{2,1,0:T(8,128)(2,1)} %bitcast.22, bf16[24,12,128,128]{3,2,1,0:T(8,128)(2,1)} %bitcast.19, ...), custom_call_target="tpu_custom_call" | custom-call | tf_op jit(solution)/shard_map/exchange/pallas_call | solution.py:417
  213.2 19.8 %update.1 = (bf16[24,12,128,128]{3,2,1,0:T(8,128)(2,1)}, bf16[24,32,128]{2,1,0:T(8,128)(2,1)}) custom-call(s32[104]{0:T(128)} %concatenate.3.tab, bf16[24,12,128,128]{3,2,1,0:T(8,128)(2,1)} %bitcast.20, bf16[4,2,4,4,4,64,128]{6,5,4,3,2,1,0:T(8,128)(2,1)} %get-tuple-element.7.arr, bf16[4,3,2,128,512]{4,3,2,1,0:T(8,128)(2,1)} %get-tuple-element.8.prow, ...), custom_call_target="tpu_custom_call" | custom-call | tf_op jit(solution)/shard_map/update/pallas_call | solution.py:454
  (10 shorter events, 0.1 us)

commit v2 on v1

v2 whole, which is shorter than its diff:
```python
import jax
import jax.numpy as jnp
from jax import lax
from jax.experimental import pallas as pl
from jax.experimental.pallas import tpu as pltpu
from jax.sharding import PartitionSpec as P

MESH = pl.DeviceIdType.MESH
BF = jnp.bfloat16
F32 = jnp.float32
ROWS = [(1, 0), (3, 0), (1, 1), (3, 1), (2, 0), (2, 1), (0, 1)]
RING = [1, 3, 2]
N_SEMS = 256
KERNEL_VMEM = 46 << 20


def tables(parent_tile, row, col):
    ids = jnp.arange(128, dtype=jnp.int32)
    same = ((ids[:, None] - ids[None, :]) % 8 == 0) & ((parent_tile[:, None] - parent_tile[None, :]) % 8 == 0)
    rank = jnp.any(same & (ids[None, :] < ids[:, None]), axis=1).astype(jnp.int32)[None, :]
    e = jnp.arange(128, dtype=jnp.int32)[:, None]
    a, to = ids[None, :], parent_tile[None, :]
    sent_row = (a % 8 == row) & (to % 8 == e // 2) & (rank == e % 2)
    sent_col = (a % 16 == col) & (to % 16 == e - T_COL)
    got_row = to == row + 8 * ((e - T_RFROM) % 24)
    got_col = to == col + 16 * ((e - T_CFROM) % 12)
    hit = jnp.where(e < T_COL, sent_row, jnp.where(e < T_RFROM, sent_col, jnp.where(e < T_CFROM, got_row, got_col)))
    got_panel = (a % 16 == col) & (to == (e - T_PFROM) % 4)
    hit = jnp.where(e < T_PFROM, hit, got_panel)
    row_value = jnp.where(e < T_ROK, rank * 8 + a % 8, 1)
    col_value = jnp.where(e < T_COK, a % 16, 1)
    value = jnp.where(
        e < T_COL, a // 8, jnp.where(e < T_RFROM, a // 16, jnp.where(e < T_CFROM, row_value, col_value))
    )
    value = jnp.where(e < T_PFROM, value, jnp.where(e < T_POK, a // 16, 1))
    return jnp.sum(jnp.where(hit, value, 0), axis=1)


T_COL, T_RFROM, T_ROK, T_CFROM, T_COK, T_PFROM, T_POK = 16, 32, 56, 80, 92, 104, 108


def arrived_place(tab, i, j):
    source_row, source = tab[T_RFROM + i], tab[T_CFROM + j]
    half = source_row % 8 // 4
    major = jnp.where(half == 0, source % 4, source // 4)
    minor = jnp.where(half == 0, source // 4, source % 4)
    return source_row // 8, half, source_row % 4, major, minor, (tab[T_ROK + i] * tab[T_COK + j]) == 1


def exchange(
    tab, u, gt, front, dinv, arr, prow, pcol,
    us, ux, g1s, g1r, rowg, rowt, cmid, colt, colgr, colga, colgb, uf, sc, s1, mid, pst, psp, ra, sa, ra2, rb, sb, rb2,
    eq, fe, pp, lsem, ssem, rsem,
):
    r, c = lax.axis_index("row"), lax.axis_index("col")
    x, k, z, y = r // 2, r % 2, c // 4, c % 4
    counter = [0]
    pending = []

    def row_dev(dx, dk):
        return ((x + dx) % 4) * 2 + (k + dk) % 2

    def row_from(dx, dk):
        return ((x + 4 - dx) % 4) * 2 + (k + dk) % 2

    def sem(count=1):
        counter[0] += count
        return counter[0] - count

    def remote(src, dst, n_send, n_recv, dev):
        return pltpu.make_async_remote_copy(
            src, dst, ssem.at[n_send], rsem.at[n_recv], device_id=dev, device_id_type=MESH
        )

    def send(src, dst, dev, landing):
        n = sem()
        out = remote(src, dst, n, n, dev)
        out.start()
        pending.append(out)
        return remote(landing, landing, n, n, dev)

    def arrive(waits):
        for w in waits:
            w.wait_recv()

    def local(src, dst):
        n = sem()
        copy = pltpu.make_async_copy(src, dst, lsem.at[n])
        copy.start()
        return copy

    def at_z(n):
        return (r, n * 4 + y)

    def to_z(d):
        return at_z((z + d) % 4)

    def to_y(d):
        return (r, z * 4 + (y + d) % 4)

    load = local(u, s1.at[0:2])
    for rp in range(8):
        g1s[rp, 0] = gt[tab[2 * rp]]
        g1s[rp, 1] = gt[tab[2 * rp + 1]]
        g1s[rp, 2] = gt[2 * rp]
        g1s[rp, 3] = gt[2 * rp + 1]

    barrier = pltpu.get_barrier_semaphore()
    for dx, dk in ROWS:
        pl.semaphore_signal(barrier, inc=1, device_id=(row_dev(dx, dk), c), device_id_type=MESH)
    for d in RING:
        pl.semaphore_signal(barrier, inc=1, device_id=to_z(d), device_id_type=MESH)
        pl.semaphore_signal(barrier, inc=1, device_id=to_y(d), device_id_type=MESH)
    pl.semaphore_wait(barrier, 13)

    g1 = [
        send(g1s.at[row_dev(dx, dk)], g1r.at[r], (row_dev(dx, dk), c), g1r.at[row_from(dx, dk)])
        for dx, dk in ROWS
    ]
    g1r[r] = g1s[r]
    def send_child(part, which=ROWS):
        rank, rows = part // 2, pl.ds((part % 2) * 512, 512)
        return [
            send(
                us.at[row_dev(dx, dk), rank, rows], ux.at[r, rank, rows], (row_dev(dx, dk), c),
                ux.at[row_from(dx, dk), rank, rows],
            )
            for dx, dk in which
        ]

    spread_sems = sem(4)

    def spread(d):
        return remote(front.at[d, :, :, 0], eq, spread_sems + d, spread_sems + d, at_z(d))

    arrive(g1)
    yz, zy = pl.ds((y * 4 + z) * 32, 32), pl.ds((z * 4 + y) * 32, 32)
    y128, z128 = pl.ds(y * 128, 128), pl.ds(z * 128, 128)

    def col_piece(zp):
        return g1r.at[pl.ds(4 * (zp % 2), 4), 2 + zp // 2]

    def rows_one(rank):
        top, low = rowg.at[rank, 0:4], rowg.at[rank, 4:8]
        waits_a, waits_b = [], []
        for d in RING:
            got = pl.ds((y * 4 + (z + 4 - d) % 4) * 32, 32)
            waits_a.append(send(g1r.at[0:4, rank], top.at[:, yz], to_z(d), top.at[:, got]))
            got = pl.ds((z * 4 + (y + 4 - d) % 4) * 32, 32)
            waits_b.append(send(g1r.at[4:8, rank], low.at[:, zy], to_y(d), low.at[:, got]))
        own = [local(g1r.at[0:4, rank], top.at[:, yz]), local(g1r.at[4:8, rank], low.at[:, zy])]
        return waits_a, waits_b, own

    def rows_two(rank, first):
        top, low = rowg.at[rank, 0:4], rowg.at[rank, 4:8]
        for copy in first[2]:
            copy.wait()
        waits = []
        arrive(first[0])
        for d in RING:
            got = pl.ds((y + 4 - d) % 4 * 128, 128)
            waits.append(send(top.at[:, y128], top.at[:, y128], to_y(d), top.at[:, got]))
        arrive(first[1])
        for d in RING:
            got = pl.ds((z + 4 - d) % 4 * 128, 128)
            waits.append(send(low.at[:, z128], low.at[:, z128], to_z(d), low.at[:, got]))
        return waits

    c1 = [send(col_piece((z + d) % 4), cmid.at[z], to_z(d), cmid.at[(z + 4 - d) % 4]) for d in RING]
    own = local(col_piece(z), cmid.at[z])
    g0 = rows_one(0)
    load.wait()

    @pl.loop(0, 16)
    def _(n):
        t = tab[n]
        us[n // 2, n % 2] = s1[t // 8, t // 4 % 2, t % 4].reshape(1024, 128)

    child = {0: send_child(0, ROWS[:4])}
    ux[r] = us[r]
    own.wait()
    arrive(c1)
    c2 = [send(cmid.at[:, (y + d) % 4], colt.at[y], to_y(d), colt.at[(y + 4 - d) % 4]) for d in RING]
    mine = local(cmid.at[:, y], colt.at[y])
    g0 = rows_two(0, g0)
    child[0] += send_child(0, ROWS[4:])
    g1 = rows_one(1)
    mine.wait()
    arrive(c2)
    d1 = [send(colt, colgr.at[r], (row_dev(d, 0), c), colgr.at[row_from(d, 0)]) for d in RING]
    local(colt, colgr.at[r]).wait()
    arrive(d1)
    sibling = (row_dev(0, 1), c)
    d2 = [send(colgr.at[2 * q + k], colgr.at[2 * q + k], sibling, colgr.at[2 * q + 1 - k]) for q in range(4)]
    g1 = rows_two(1, g1)
    child[1] = send_child(1)
    arrive(d2)

    @pl.when(z == 0)
    def _():
        for d in (1, 2, 3):
            spread(d).start()
        copy = pltpu.make_async_copy(front.at[0, :, :, 0], eq, lsem.at[N_SEMS - 1])
        copy.start()
        copy.wait()

    for j in range(8):
        for a in range(4):
            for b in range(4):
                piece = colgr[j, a, b]
                colga[pl.ds((a * 4 + b) * 32, 32), pl.ds(j * 128, 128)] = piece
                colgb[pl.ds((b * 4 + a) * 32, 32), pl.ds(j * 128, 128)] = piece

    def turn(rank):
        @pl.loop(0, 8)
        def _(q):
            turned = rowg[rank, q].T
            rowt[2 * rank, q] = turned[0:64]
            rowt[2 * rank + 1, q] = turned[64:128]

    def schur(part, half):
        rank = part // 2
        colg = colga if half == 0 else colgb

        @pl.loop(0, 4)
        def _(q):
            uf[pl.ds(q * 512, 512)] = ux[half * 4 + q, rank, pl.ds((part % 2) * 512, 512)].astype(F32)

        left = rowt.at[part, pl.ds(half * 4, 4)]

        for n in range(4):
            prod = jnp.dot(
                left[...].reshape(256, 512), colg[:, n * 256 : n * 256 + 256], preferred_element_type=F32
            )
            for e in range(2):
                j = 2 * n + e
                sc[j] = (uf[pl.ds(j, 256, stride=8), :] - prod[:, e * 128 : e * 128 + 128]).astype(BF)

        @pl.loop(0, 16)
        def _(t):
            lo, hi = t // 4, t % 4
            if half == 0:
                s1[part, half, lo, hi] = sc[tab[T_COL + t]]
            else:
                s1[part, half, hi, lo] = sc[tab[T_COL + t]]

        for t in range(4):
            tile = sc[tab[T_PFROM + t]]
            tile = jnp.where(tab[T_POK + t] == 1, tile, jnp.zeros_like(tile)).reshape(4, 64, 128)
            pst[part, half, :, :, t * 128 : t * 128 + 128] = tile

    copies = []

    def step_one(part):
        for half in range(2):
            one[part, half] = step_half(part, half)

    def step_half(part, half):
        me, to = (z, to_z) if half == 0 else (y, to_y)
        waits = [
            send(s1.at[part, half, (me + d) % 4], mid.at[part, half, me], to(d), mid.at[part, half, (me + 4 - d) % 4])
            for d in RING
        ]
        return waits, local(s1.at[part, half, me], mid.at[part, half, me])

    def step_two(part):
        for half in range(2):
            arrive(one[part, half][0])
            one[part, half][1].wait()
            me, to = (y, to_y) if half == 0 else (z, to_z)
            for d in RING:
                two.append(
                    send(
                        mid.at[part, half, :, (me + d) % 4], arr.at[part, half, me], to(d),
                        arr.at[part, half, (me + 4 - d) % 4],
                    )
                )
            copies.append(local(mid.at[part, half, :, me], arr.at[part, half, me]))

    one, two = {}, []

    def make(part):
        if part % 2 == 0:
            arrive(g0 if part == 0 else g1)
            turn(part // 2)
        arrive(child[part])
        for half in range(2):
            schur(part, half)
        if part + 2 < 4:
            child[part + 2] = send_child(part + 2)

    make(0)
    step_one(0)
    lanes = pl.ds(pl.multiple_of(y * 128, 128), 128)
    for d in (1, 2, 3):

        @pl.when(z == 0)
        def _():
            spread(d).wait_send()

        @pl.when(z == d)
        def _():
            spread(d).wait_recv()

    e1 = [
        send(
            eq.at[:, :, pl.ds((y + d) % 4 * 32, 32)], fe.at[:, :, :, lanes], to_y(d),
            fe.at[:, :, :, pl.ds(pl.multiple_of((y + 4 - d) % 4 * 128, 128), 128)],
        )
        for d in RING
    ]
    copies.append(local(eq.at[:, :, pl.ds(y * 32, 32)], fe.at[:, :, :, lanes]))
    make(1)
    step_one(1)
    step_two(0)
    make(2)
    make(3)

    @pl.loop(0, 24)
    def _(i):
        source_row = tab[T_RFROM + i]
        rank, half = source_row // 8, source_row % 8 // 4
        place = source_row % 4
        tile = jnp.concatenate([pst[rank * 2, half, place], pst[rank * 2 + 1, half, place]], axis=0)
        psp[i // 6, i % 6 // 2, i % 2] = jnp.where(tab[T_ROK + i] == 1, tile, jnp.zeros_like(tile))

    y32 = pl.ds(pl.multiple_of(y * 32, 32), 32)
    f1, f2 = [], []
    for n, d in enumerate(RING):
        f1.append(send(psp.at[(z + d) % 4, :, 0], ra.at[n], to_z(d), ra.at[n]))
        f2.append(send(psp.at[:, :, 1, pl.ds((y + d) % 4 * 32, 32)], rb.at[n], to_y(d), rb.at[n]))
    step_two(1)
    arrive(f1)
    sa[...] = psp[z, :, 0] + ra[0] + ra[1] + ra[2]
    f3 = [send(sa.at[:, pl.ds((y + d) % 4 * 32, 32)], ra2.at[n], to_y(d), ra2.at[n]) for n, d in enumerate(RING)]
    arrive(f2)
    sb[...] = psp[:, :, 1, y32] + rb[0] + rb[1] + rb[2]
    f4 = [send(sb.at[(z + d) % 4], rb2.at[n], to_z(d), rb2.at[n]) for n, d in enumerate(RING)]
    step_one(2)
    arrive(f3)
    arrive(f4)
    arrive(e1)
    copies[0].wait()
    even = sa[:, y32] + ra2[0] + ra2[1] + ra2[2]
    odd = sb[z] + rb2[0] + rb2[1] + rb2[2]
    even = (fe[:, 0].astype(F32) + even.astype(F32)).astype(BF).reshape(96, 512)
    odd = (fe[:, 1].astype(F32) + odd.astype(F32)).astype(BF).reshape(96, 512)
    pp[:, 0] = jnp.dot(even, dinv[...], preferred_element_type=F32).astype(BF).reshape(3, 32, 512)
    pp[:, 1] = jnp.dot(odd, dinv[...], preferred_element_type=F32).astype(BF).reshape(3, 32, 512)
    own = local(pp, prow.at[z, :, :, y32])
    p1, p2 = [], []
    for d in RING:
        p1.append(send(pp.at[:, 0], prow.at[z, :, 0, y32], to_z(d), prow.at[(z + 4 - d) % 4, :, 0, y32]))
        p2.append(send(pp.at[:, 1], prow.at[z, :, 1, y32], to_y(d), prow.at[z, :, 1, pl.ds((y + 4 - d) % 4 * 32, 32)]))
    own.wait()
    step_one(3)
    arrive(p1)
    p3 = [
        send(prow.at[:, :, 0, y32], prow.at[:, :, 0, y32], to_y(d), prow.at[:, :, 0, pl.ds((y + 4 - d) % 4 * 32, 32)])
        for d in RING
    ]
    arrive(p2)
    p4 = [send(prow.at[z, :, 1], prow.at[z, :, 1], to_z(d), prow.at[(z + 4 - d) % 4, :, 1]) for d in RING]
    step_two(2)
    arrive(p3)
    arrive(p4)

    root = c % 8
    upper = c // 8
    n_in = sem()
    n_out = [sem() for _ in ROWS]

    def piece(q):
        return pl.ds(q * 16, 16)

    def deal(dx, dk, n):
        q = row_dev(dx, dk)
        return remote(prow.at[:, :, upper, piece(q)], pcol.at[:, :, piece(q)], n, n_in, (q, c))

    @pl.when(r == root)
    def _():
        for (dx, dk), n in zip(ROWS, n_out):
            deal(dx, dk, n).start()
        copy = pltpu.make_async_copy(prow.at[:, :, upper, piece(r)], pcol.at[:, :, piece(r)], lsem.at[N_SEMS - 2])
        copy.start()
        copy.wait()
        for (dx, dk), n in zip(ROWS, n_out):
            deal(dx, dk, n).wait_send()

    @pl.when(r != root)
    def _():
        remote(pcol.at[:, :, piece(r)], pcol.at[:, :, piece(r)], n_in, n_in, (r, c)).wait_recv()

    q1 = [
        send(
            pcol.at[:, :, piece(r)], pcol.at[:, :, piece(r)], (row_dev(d, 0), c), pcol.at[:, :, piece(row_from(d, 0))]
        )
        for d in RING
    ]
    step_two(3)
    arrive(q1)
    q2 = [
        send(
            pcol.at[:, :, piece(2 * q + k)], pcol.at[:, :, piece(2 * q + k)], sibling,
            pcol.at[:, :, piece(2 * q + 1 - k)],
        )
        for q in range(4)
    ]

    arrive(q2)
    arrive(two)
    for copy in copies[1:]:
        copy.wait()
    for copy in pending:
        copy.wait_send()


def update(tab, front, *refs):
    arrs, (prow, pcol, out, panel, right) = refs[:4], refs[4:]
    r, c = lax.axis_index("row"), lax.axis_index("col")
    step = pl.program_id(0)

    @pl.when(step == 0)
    def _():
        for j in range(12):
            tile = pcol[j // 3, j % 3]
            if j == 0:
                tile = jnp.where(c >= 4, tile, jnp.zeros_like(tile))
            right[:, j * 128 : j * 128 + 128] = tile.T

    rows = prow[...].reshape(256, 512)
    pick = (lax.broadcasted_iota(jnp.int32, (32, 512), 1) - 32 * c) == lax.broadcasted_iota(jnp.int32, (32, 512), 0)
    chosen = lax.dot_general(
        jnp.where(pick, 1.0, 0.0).astype(BF), rows, (((1,), (1,)), ((), ())), preferred_element_type=F32
    ).astype(BF)
    panel[0] = chosen[:, 0:128]
    panel[1] = chosen[:, 128:256]
    trailing = jnp.logical_or(step > 0, r >= 4)
    rows = jnp.concatenate([jnp.where(trailing, rows[0:128], jnp.zeros_like(rows[0:128])), rows[128:256]], axis=0)
    for n in range(6):
        prod = jnp.dot(rows, right[:, n * 256 : n * 256 + 256], preferred_element_type=F32)
        for e in range(2):
            for b in range(2):
                j = 2 * n + e
                _, _, _, major, minor, ok = arrived_place(tab, 2 * step + b, j)
                for p in range(2):
                    tile = arrs[2 * b + p][0, 0, major, minor]
                    lines = slice(p * 64, p * 64 + 64)
                    ext = (
                        front[b, j, lines].astype(F32) + jnp.where(ok, tile, jnp.zeros_like(tile)).astype(F32)
                    ).astype(BF)
                    term = prod[b * 128 + p * 64 : b * 128 + p * 64 + 64, e * 128 : e * 128 + 128]
                    out[b, j, lines] = (ext.astype(F32) - term).astype(BF)


def arrivals(b, p):
    def index(step, tab):
        source_row = tab[T_RFROM + 2 * step + b]
        return (source_row // 8 * 2 + p, source_row % 8 // 4, 0, 0, source_row % 4, 0)

    return pl.BlockSpec((1, 1, 4, 4, 64, 128), index)


def body(child_update, child_panel, front, diag_inverse, parent_tile):
    tab = tables(parent_tile, lax.axis_index("row"), lax.axis_index("col"))
    u = child_update.reshape(2, 2, 4, 4, 256, 128)
    gt = child_panel.reshape(16, 128, 32).transpose(0, 2, 1)
    tiles = front.reshape(24, 128, 12, 128).transpose(0, 2, 1, 3)
    vmem, anywhere = pl.BlockSpec(memory_space=pltpu.VMEM), pl.BlockSpec(memory_space=pl.ANY)
    smem = pl.BlockSpec(memory_space=pltpu.SMEM)
    arr, prow, pcol = pl.pallas_call(
        exchange,
        out_shape=(
            jax.ShapeDtypeStruct((4, 2, 4, 4, 256, 128), BF),
            jax.ShapeDtypeStruct((4, 3, 2, 128, 512), BF),
            jax.ShapeDtypeStruct((4, 3, 128, 512), BF),
        ),
        in_specs=[smem, anywhere, vmem, anywhere, vmem],
        out_specs=(anywhere, anywhere, anywhere),
        scratch_shapes=[
            pltpu.VMEM((8, 2, 1024, 128), BF),
            pltpu.VMEM((8, 2, 1024, 128), BF),
            pltpu.VMEM((8, 4, 32, 128), BF),
            pltpu.VMEM((8, 4, 32, 128), BF),
            pltpu.VMEM((2, 8, 512, 128), BF),
            pltpu.VMEM((4, 8, 64, 512), BF),
            pltpu.VMEM((4, 4, 32, 128), BF),
            pltpu.VMEM((4, 4, 32, 128), BF),
            pltpu.VMEM((8, 4, 4, 32, 128), BF),
            pltpu.VMEM((512, 1024), BF),
            pltpu.VMEM((512, 1024), BF),
            pltpu.VMEM((2048, 128), F32),
            pltpu.VMEM((8, 256, 128), BF),
            pltpu.VMEM((4, 2, 4, 4, 256, 128), BF),
            pltpu.VMEM((4, 2, 4, 4, 256, 128), BF),
            pltpu.VMEM((4, 2, 4, 64, 512), BF),
            pltpu.VMEM((4, 3, 2, 128, 512), BF),
            pltpu.VMEM((3, 3, 128, 512), BF),
            pltpu.VMEM((3, 128, 512), BF),
            pltpu.VMEM((3, 3, 32, 512), BF),
            pltpu.VMEM((3, 4, 3, 32, 512), BF),
            pltpu.VMEM((4, 3, 32, 512), BF),
            pltpu.VMEM((3, 3, 32, 512), BF),
            pltpu.VMEM((3, 2, 128, 128), BF),
            pltpu.VMEM((3, 2, 32, 512), BF),
            pltpu.VMEM((3, 2, 32, 512), BF),
            pltpu.SemaphoreType.DMA((N_SEMS,)),
            pltpu.SemaphoreType.DMA((N_SEMS,)),
            pltpu.SemaphoreType.DMA((N_SEMS,)),
        ],
        compiler_params=pltpu.CompilerParams(collective_id=0, has_side_effects=True, vmem_limit_bytes=KERNEL_VMEM),
        name="exchange",
    )(tab, u, gt, tiles.reshape(4, 3, 2, 12, 128, 128), diag_inverse)
    updated, panel = pl.pallas_call(
        update,
        grid_spec=pltpu.PrefetchScalarGridSpec(
            num_scalar_prefetch=1,
            grid=(12,),
            in_specs=[
                pl.BlockSpec((2, 12, 128, 128), lambda s, t: (s, 0, 0, 0)),
                arrivals(0, 0),
                arrivals(0, 1),
                arrivals(1, 0),
                arrivals(1, 1),
                pl.BlockSpec((1, 1, 2, 128, 512), lambda s, t: (s // 3, s % 3, 0, 0, 0)),
                pl.BlockSpec((4, 3, 128, 512), lambda s, t: (0, 0, 0, 0)),
            ],
            out_specs=[
                pl.BlockSpec((2, 12, 128, 128), lambda s, t: (s, 0, 0, 0)),
                pl.BlockSpec((2, 32, 128), lambda s, t: (s, 0, 0)),
            ],
            scratch_shapes=[pltpu.VMEM((512, 1536), BF)],
        ),
        out_shape=(jax.ShapeDtypeStruct((24, 12, 128, 128), BF), jax.ShapeDtypeStruct((24, 32, 128), BF)),
        compiler_params=pltpu.CompilerParams(vmem_limit_bytes=46 << 20),
        name="update",
    )(tab, tiles, arr, arr, arr, arr, prow, pcol)
    return (
        panel.transpose(0, 2, 1).reshape(24, 1, 128, 1, 32),
        updated.transpose(0, 2, 1, 3).reshape(24, 1, 128, 12, 1, 128),
    )


def solution(mesh):
    return jax.shard_map(
        body,
        mesh=mesh,
        in_specs=(
            P(None, "row", None, None, "col", None),
            P(None, "row", None, "col"),
            P(None, "row", None, None, "col", None),
            P(),
            P(),
        ),
        out_specs=(P(None, "row", None, "col", None), P(None, "row", None, None, "col", None)),
        check_vma=False,
    )
```

time: 234 us -> 216 us (0.923)
  the two profiles are of different devices: /device:TPU:1 before, /device:TPU:23 now
where the time goes in v2:
time: 216 us
  Pallas kernels  210 us (97%)
  other arithmetic  2.7 us (1%)
    pallas_call x1, Pallas kernels, body(): pl.pallas_call(exchange, out_shape=(jax.ShapeDtypeStruct((4, 2, 4, 4, 256...  192 us
    pallas_call x1, Pallas kernels, body(): pl.pallas_call(update, grid_spec=pltpu.PrefetchScalarGridSpec(num_scalar_...  17.8 us

profile of v2, /device:TPU:23, one launch (start us, length us, event | category | flops | bytes accessed | tf_op | source)
XLA Modules:
  0.0 215.6 jit_solution(7674457756010336680)
XLA Ops:
  0.6 0.9 fusion.9
  1.6 0.7 and_select_fusion.9
  2.4 1.0 select_reduce_fusion.tab
  3.4 0.0 copy-start
  3.4 1.0 copy-done
  4.4 0.0 copy-start.1
  4.5 0.9 copy-done.1
  5.4 192.4 %exchange.1 = (bf16[4,2,4,4,256,128]{5,4,3,2,1,0:T(8,128)(2,1)}, bf16[4,3,2,128,512]{4,3,2,1,0:T(8,128)(2,1)S(1)}, bf16[4,3,128,512]{3,2,1,0:T(8,128)(2,1)S(1)}) custom-call(s32[128]{0:T(128)S(1)} %select_reduce_fusion.tab, bf16[2,2,4,4,256,128]{5,4,3,2,1,0:T(8,128)(2,1)} %bitcast.22, bf16[16,32,128]{2,1,0:T(8,128)(2,1)S(1)} %bitcast.19, ...), custom_call_target="tpu_custom_call" | custom-call | tf_op jit(solution)/shard_map/exchange/pallas_call | solution.py:471
  197.7 17.8 %update.1 = (bf16[24,12,128,128]{3,2,1,0:T(8,128)(2,1)}, bf16[24,32,128]{2,1,0:T(8,128)(2,1)}) custom-call(s32[128]{0:T(128)S(1)} %select_reduce_fusion.tab, bf16[24,12,128,128]{3,2,1,0:T(8,128)(2,1)} %bitcast.21, bf16[4,2,4,4,256,128]{5,4,3,2,1,0:T(8,128)(2,1)} %get-tuple-element.7.refs_0_.refs_1_.refs_2_.refs_3_, ...), custom_call_target="tpu_custom_call" | custom-call | tf_op jit(solution)/shard_map/update/pallas_call | solution.py:514
  (11 shorter events, 0.1 us)
Async XLA Ops:
  3.4 1.0 copy-start
  4.4 0.9 copy-start.1

commit v3 on v2

--- a/solution.py
+++ b/solution.py
@@ -118,6 +118,18 @@
         for dx, dk in ROWS
     ]
     g1r[r] = g1s[r]
+
+    spread_sems = sem(4)
+
+    def spread(d):
+        return remote(front.at[d, :, :, 0], eq, spread_sems + d, spread_sems + d, at_z(d))
+
+    @pl.when(z == 0)
+    def _():
+        for d in (1, 2, 3):
+            spread(d).start()
+        copy = pltpu.make_async_copy(front.at[0, :, :, 0], eq, lsem.at[N_SEMS - 1])
+        copy.start()
     def send_child(part, which=ROWS):
         rank, rows = part // 2, pl.ds((part % 2) * 512, 512)
         return [
@@ -127,11 +139,6 @@
             )
             for dx, dk in which
         ]
-
-    spread_sems = sem(4)
-
-    def spread(d):
-        return remote(front.at[d, :, :, 0], eq, spread_sems + d, spread_sems + d, at_z(d))
 
     arrive(g1)
     yz, zy = pl.ds((y * 4 + z) * 32, 32), pl.ds((z * 4 + y) * 32, 32)
@@ -188,21 +195,33 @@
     mine.wait()
     arrive(c2)
     d1 = [send(colt, colgr.at[r], (row_dev(d, 0), c), colgr.at[row_from(d, 0)]) for d in RING]
+    lanes = pl.ds(pl.multiple_of(y * 128, 128), 128)
+    for d in (1, 2, 3):
+
+        @pl.when(z == 0)
+        def _():
+            spread(d).wait_send()
+            if d == 1:
+                pltpu.make_async_copy(front.at[0, :, :, 0], eq, lsem.at[N_SEMS - 1]).wait()
+
+        @pl.when(z == d)
+        def _():
+            spread(d).wait_recv()
+
+    e1 = [
+        send(
+            eq.at[:, :, pl.ds((y + d) % 4 * 32, 32)], fe.at[:, :, :, lanes], to_y(d),
+            fe.at[:, :, :, pl.ds(pl.multiple_of((y + 4 - d) % 4 * 128, 128), 128)],
+        )
+        for d in RING
+    ]
+    own_fe = local(eq.at[:, :, pl.ds(y * 32, 32)], fe.at[:, :, :, lanes])
     local(colt, colgr.at[r]).wait()
     arrive(d1)
     sibling = (row_dev(0, 1), c)
     d2 = [send(colgr.at[2 * q + k], colgr.at[2 * q + k], sibling, colgr.at[2 * q + 1 - k]) for q in range(4)]
-    g1 = rows_two(1, g1)
     child[1] = send_child(1)
     arrive(d2)
-
-    @pl.when(z == 0)
-    def _():
-        for d in (1, 2, 3):
-            spread(d).start()
-        copy = pltpu.make_async_copy(front.at[0, :, :, 0], eq, lsem.at[N_SEMS - 1])
-        copy.start()
-        copy.wait()
 
     for j in range(8):
         for a in range(4):
@@ -291,25 +310,7 @@
 
     make(0)
     step_one(0)
-    lanes = pl.ds(pl.multiple_of(y * 128, 128), 128)
-    for d in (1, 2, 3):
-
-        @pl.when(z == 0)
-        def _():
-            spread(d).wait_send()
-
-        @pl.when(z == d)
-        def _():
-            spread(d).wait_recv()
-
-    e1 = [
-        send(
-            eq.at[:, :, pl.ds((y + d) % 4 * 32, 32)], fe.at[:, :, :, lanes], to_y(d),
-            fe.at[:, :, :, pl.ds(pl.multiple_of((y + 4 - d) % 4 * 128, 128), 128)],
-        )
-        for d in RING
-    ]
-    copies.append(local(eq.at[:, :, pl.ds(y * 32, 32)], fe.at[:, :, :, lanes]))
+    g1 = rows_two(1, g1)
     make(1)
     step_one(1)
     step_two(0)
@@ -340,7 +341,7 @@
     arrive(f3)
     arrive(f4)
     arrive(e1)
-    copies[0].wait()
+    own_fe.wait()
     even = sa[:, y32] + ra2[0] + ra2[1] + ra2[2]
     odd = sb[z] + rb2[0] + rb2[1] + rb2[2]
     even = (fe[:, 0].astype(F32) + even.astype(F32)).astype(BF).reshape(96, 512)
@@ -409,14 +410,14 @@
 
     arrive(q2)
     arrive(two)
-    for copy in copies[1:]:
+    for copy in copies:
         copy.wait()
     for copy in pending:
         copy.wait_send()
 
 
 def update(tab, front, *refs):
-    arrs, (prow, pcol, out, panel, right) = refs[:4], refs[4:]
+    arrs, (prow, pcol, out, panel, right) = refs[:8], refs[8:]
     r, c = lax.axis_index("row"), lax.axis_index("col")
     step = pl.program_id(0)
 
@@ -428,21 +429,21 @@
                 tile = jnp.where(c >= 4, tile, jnp.zeros_like(tile))
             right[:, j * 128 : j * 128 + 128] = tile.T
 
-    rows = prow[...].reshape(256, 512)
+    rows = prow[...].reshape(512, 512)
     pick = (lax.broadcasted_iota(jnp.int32, (32, 512), 1) - 32 * c) == lax.broadcasted_iota(jnp.int32, (32, 512), 0)
     chosen = lax.dot_general(
         jnp.where(pick, 1.0, 0.0).astype(BF), rows, (((1,), (1,)), ((), ())), preferred_element_type=F32
     ).astype(BF)
-    panel[0] = chosen[:, 0:128]
-    panel[1] = chosen[:, 128:256]
+    for b in range(4):
+        panel[b] = chosen[:, b * 128 : b * 128 + 128]
     trailing = jnp.logical_or(step > 0, r >= 4)
-    rows = jnp.concatenate([jnp.where(trailing, rows[0:128], jnp.zeros_like(rows[0:128])), rows[128:256]], axis=0)
+    rows = jnp.concatenate([jnp.where(trailing, rows[0:128], jnp.zeros_like(rows[0:128])), rows[128:512]], axis=0)
     for n in range(6):
         prod = jnp.dot(rows, right[:, n * 256 : n * 256 + 256], preferred_element_type=F32)
         for e in range(2):
-            for b in range(2):
+            for b in range(4):
                 j = 2 * n + e
-                _, _, _, major, minor, ok = arrived_place(tab, 2 * step + b, j)
+                _, _, _, major, minor, ok = arrived_place(tab, 4 * step + b, j)
                 for p in range(2):
                     tile = arrs[2 * b + p][0, 0, major, minor]
                     lines = slice(p * 64, p * 64 + 64)
@@ -455,7 +456,7 @@
 
 def arrivals(b, p):
     def index(step, tab):
-        source_row = tab[T_RFROM + 2 * step + b]
+        source_row = tab[T_RFROM + 4 * step + b]
         return (source_row // 8 * 2 + p, source_row % 8 // 4, 0, 0, source_row % 4, 0)
 
     return pl.BlockSpec((1, 1, 4, 4, 64, 128), index)
@@ -515,26 +516,23 @@
         update,
         grid_spec=pltpu.PrefetchScalarGridSpec(
             num_scalar_prefetch=1,
-            grid=(12,),
+            grid=(6,),
             in_specs=[
-                pl.BlockSpec((2, 12, 128, 128), lambda s, t: (s, 0, 0, 0)),
-                arrivals(0, 0),
-                arrivals(0, 1),
-                arrivals(1, 0),
-                arrivals(1, 1),
-                pl.BlockSpec((1, 1, 2, 128, 512), lambda s, t: (s // 3, s % 3, 0, 0, 0)),
+                pl.BlockSpec((4, 12, 128, 128), lambda s, t: (s, 0, 0, 0)),
+                *[arrivals(b, p) for b in range(4) for p in range(2)],
+                pl.BlockSpec((4, 128, 512), lambda s, t: (s, 0, 0)),
                 pl.BlockSpec((4, 3, 128, 512), lambda s, t: (0, 0, 0, 0)),
             ],
             out_specs=[
-                pl.BlockSpec((2, 12, 128, 128), lambda s, t: (s, 0, 0, 0)),
-                pl.BlockSpec((2, 32, 128), lambda s, t: (s, 0, 0)),
+                pl.BlockSpec((4, 12, 128, 128), lambda s, t: (s, 0, 0, 0)),
+                pl.BlockSpec((4, 32, 128), lambda s, t: (s, 0, 0)),
             ],
             scratch_shapes=[pltpu.VMEM((512, 1536), BF)],
         ),
         out_shape=(jax.ShapeDtypeStruct((24, 12, 128, 128), BF), jax.ShapeDtypeStruct((24, 32, 128), BF)),
         compiler_params=pltpu.CompilerParams(vmem_limit_bytes=46 << 20),
         name="update",
-    )(tab, tiles, arr, arr, arr, arr, prow, pcol)
+    )(tab, tiles, *[arr] * 8, prow.reshape(24, 128, 512), pcol)
     return (
         panel.transpose(0, 2, 1).reshape(24, 1, 128, 1, 32),
         updated.transpose(0, 2, 1, 3).reshape(24, 1, 128, 12, 1, 128),

time: 216 us -> 211 us (0.977)
  the two profiles are of different devices: /device:TPU:23 before, /device:TPU:1 now
where the time goes in v3:
time: 211 us
  Pallas kernels  206 us (98%)
  other arithmetic  2.7 us (1%)
    pallas_call x1, Pallas kernels, body(): pl.pallas_call(exchange, out_shape=(jax.ShapeDtypeStruct((4, 2, 4, 4, 256...  190 us
    pallas_call x1, Pallas kernels, body(): pl.pallas_call(update, grid_spec=pltpu.PrefetchScalarGridSpec(num_scalar_...  15.7 us

profile of v3, /device:TPU:1, one launch (start us, length us, event | category | flops | bytes accessed | tf_op | source)
XLA Modules:
  0.0 211.2 jit_solution(14643516427988118440)
XLA Ops:
  0.6 0.9 fusion.9
  1.6 0.7 and_select_fusion.9
  2.4 1.0 select_reduce_fusion.tab
  3.4 0.0 copy-start
  3.4 1.0 copy-done
  4.4 0.0 copy-start.1
  4.5 0.9 copy-done.1
  5.4 190.1 %exchange.1 = (bf16[4,2,4,4,256,128]{5,4,3,2,1,0:T(8,128)(2,1)}, bf16[4,3,2,128,512]{4,3,2,1,0:T(8,128)(2,1)S(1)}, bf16[4,3,128,512]{3,2,1,0:T(8,128)(2,1)S(1)}) custom-call(s32[128]{0:T(128)S(1)} %select_reduce_fusion.tab, bf16[2,2,4,4,256,128]{5,4,3,2,1,0:T(8,128)(2,1)} %bitcast.24, bf16[16,32,128]{2,1,0:T(8,128)(2,1)S(1)} %bitcast.21, ...), custom_call_target="tpu_custom_call" | custom-call | tf_op jit(solution)/shard_map/exchange/pallas_call | solution.py:472
  195.4 15.7 %update.1 = (bf16[24,12,128,128]{3,2,1,0:T(8,128)(2,1)}, bf16[24,32,128]{2,1,0:T(8,128)(2,1)}) custom-call(s32[128]{0:T(128)S(1)} %select_reduce_fusion.tab, bf16[24,12,128,128]{3,2,1,0:T(8,128)(2,1)} %bitcast.23, bf16[4,2,4,4,256,128]{5,4,3,2,1,0:T(8,128)(2,1)} %get-tuple-element.7.refs_0_.refs_1_.refs_2_.refs_3_.refs_4_.refs_5_.refs_6_.refs_7_, ...), custom_call_target="tpu_custom_call" | custom-call | tf_op jit(solution)/shard_map/update/pallas_call | solution.py:515
  (11 shorter events, 0.1 us)
Async XLA Ops:
  3.4 1.0 copy-start
  4.4 0.9 copy-start.1
